TPU v7x, 256 devices: a whole 4x4x8 slice. The times are simulated.
256 devices in a mesh: hist: 8 (over z), cand: 32 (over x, y, core).
Axes of the slice: x: 4, y: 4, z: 8, core: 2. Of those that a mesh axis runs over, the one named last changes fastest.
Arguments:
- candidates: bfloat16 [32, 256, 1024], P('cand'), may hold values from -6 to 6
- input_gain: float32 [1024], replicated, may hold values from 0.1 to 1.9
- proj_weight: bfloat16 [2, 1024, 1024], P(None, None, 'hist'), may hold values from -0.1875 to 0.1875
- history_cache: bfloat16 [1280, 8, 512, 256], P('cand', 'hist'), may hold values from -6 to 6
- slot_user: int32 [1280], P('cand'), may hold values from 0 to 31
- slot_block: int32 [1280], P('cand'), may hold values from -1 to 31, as said below
- history_len: int32 [32], replicated, may hold values from 1537 to 16384
- attention_gain: float32 [1024], replicated, may hold values from 0.1 to 1.9
- out_weight: bfloat16 [1024, 1024], P(None, 'hist'), may hold values from -0.1875 to 0.1875
Outputs:
- result: bfloat16 [32, 256, 1024], P('cand', None, 'hist')
Inputs may be any that keep to these rules, and one draw needn't show every extreme that they name: Each pair of a user u and a block number b < ceil(history_len[u] / 512) is held by exactly one slot; every other slot has slot_block -1.
All inputs are finite; a program needn't handle non-finite values.
Results may differ from a plain program's by a relative error of at most 0.015.
Values may be sent and summed in bfloat16 or wider, within the bound.
A program may use at most 128 MiB of HBM per device.

v0:
```python
import jax
import jax.numpy as jnp
from jax import lax
from jax.sharding import PartitionSpec as P

D = 1024
DH = 128


def layer_norm(rows, gain):
    row_mean = jnp.mean(rows, axis=-1, keepdims=True)
    centred = rows - row_mean
    row_var = jnp.mean(centred * centred, axis=-1, keepdims=True)
    return centred * lax.rsqrt(row_var + 1e-05) * gain


def local(
    candidates,
    input_gain,
    proj_weight,
    history_cache,
    slot_user,
    slot_block,
    history_len,
    attention_gain,
    out_weight,
):
    user_count = lax.axis_size("cand")
    cand_count = candidates.shape[1]
    head_cols = proj_weight.shape[2]
    heads_here = head_cols // DH
    slot_count = history_cache.shape[0]
    block_len = history_cache.shape[2]
    cand_rows = candidates.astype(jnp.float32)
    normed_input = layer_norm(cand_rows, input_gain).astype(jnp.bfloat16)
    flat_rows = normed_input.reshape(cand_count, D)
    gate_own = jax.nn.silu(
        jnp.dot(flat_rows, proj_weight[0], preferred_element_type=jnp.float32)
    ).astype(jnp.bfloat16)
    features = lax.all_gather(normed_input, "cand", axis=0, tiled=True)
    query_all = jax.nn.silu(
        jnp.dot(
            features.reshape(user_count * cand_count, D),
            proj_weight[1],
            preferred_element_type=jnp.float32,
        )
    )
    query_all = query_all.astype(jnp.bfloat16).reshape(user_count, cand_count, head_cols)
    slot_queries = jnp.take(query_all, slot_user, axis=0).reshape(
        slot_count, cand_count, heads_here, DH
    )
    cache_keys = history_cache[..., :DH]
    cache_values = history_cache[..., DH:]
    scores = jnp.einsum(
        "schd,shtd->shct", slot_queries, cache_keys, preferred_element_type=jnp.float32
    ) * DH ** (-0.5)
    user_ids = jnp.arange(user_count, dtype=jnp.int32)
    owner_hit = slot_user[:, None] == user_ids[None, :]
    lengths = jnp.sum(jnp.where(owner_hit, history_len[None, :], 0), axis=1)
    event_index = slot_block[:, None] * block_len + jnp.arange(block_len, dtype=jnp.int32)[None, :]
    live_mask = (slot_block[:, None] >= 0) & (event_index < lengths[:, None])
    weights = (jax.nn.silu(scores) * live_mask[:, None, None, :].astype(jnp.float32)).astype(
        jnp.bfloat16
    )
    partial_value = jnp.einsum(
        "shct,shtd->schd", weights, cache_values, preferred_element_type=jnp.float32
    )
    partial_value = partial_value.reshape(slot_count, cand_count, head_cols)
    owner_table = owner_hit.astype(jnp.float32)
    buffer = jnp.einsum("su,scw->ucw", owner_table, partial_value, precision=lax.Precision.HIGHEST)
    attn_head = lax.psum_scatter(
        buffer.astype(jnp.bfloat16), "cand", scatter_dimension=0, tiled=True
    ).astype(jnp.float32)
    first_col = lax.axis_index("hist") * head_cols
    attn_all, gate_all = (
        lax.all_gather(attn_head, "hist", axis=2, tiled=True),
        lax.all_gather(
            gate_own.astype(jnp.float32).reshape(1, cand_count, head_cols),
            "hist",
            axis=2,
            tiled=True,
        ),
    )
    gated = (layer_norm(attn_all, attention_gain) * gate_all).astype(jnp.bfloat16)
    cand_cols = lax.dynamic_slice_in_dim(cand_rows, first_col, head_cols, 2)
    projected = jnp.dot(
        gated.reshape(cand_count, D), out_weight, preferred_element_type=jnp.float32
    )
    result = cand_cols + projected.reshape(1, cand_count, head_cols)
    return result.astype(jnp.bfloat16)


def solution(mesh):
    return jax.shard_map(
        local,
        mesh=mesh,
        in_specs=(
            P("cand", None, None),
            P(),
            P(None, None, "hist"),
            P("cand", "hist", None, None),
            P("cand"),
            P("cand"),
            P(),
            P(),
            P(None, "hist"),
        ),
        out_specs=P("cand", None, "hist"),
        check_vma=False,
    )
```

profile of v0, /device:TPU:1, one launch (start us, length us, event | category | flops | bytes accessed | tf_op | source)
XLA Modules:
  0.0 302.4 jit_solution(7281226300130473553)
XLA Ops:
  6.5 1.2 convert_reduce_fusion
  7.8 1.3 multiply_reduce_fusion.1
  9.1 2.1 multiply_convert_fusion.3
  11.3 0.7 compare_select_fusion
  12.0 0.8 select_reduce_fusion
  12.8 0.7 broadcast_compare_fusion
  13.4 0.7 broadcast_multiply_fusion.2
  14.1 0.7 compare_and_fusion
  14.7 0.1 fusion.41
  14.8 78.4 %all-gather.5.cloned.1.call-done = bf16[32,256,1024]{2,1,0:T(8,128)(2,1)} async-done(((bf16[1,256,1024]{2,1,0:T(8,128)(2,1)}), bf16[32,256,1024]{2,1,0:T(8,128)(2,1)}) %all-gather.5.cloned.1.call-update) | async-done | bytes 16777232 | tf_op jit(solution)/shard_map/all_gather | solution.py:40
  93.2 10.3 %multiply_convert_fusion.2 = bf16[8192,128]{1,0:T(8,128)(2,1)S(1)} fusion(bf16[8192,1024]{1,0:T(8,128)(2,1)} %bitcast.52, bf16[2,1024,128]{2,1,0:T(8,128)(2,1)} %param.11), kind=kOutput, calls=%fused_computation.8 | convolution fusion | flops 2152726528 | bytes 19136512 | tf_op jit(solution)/shard_map/dot_general | solution.py:42
  103.5 2.5 gather_fusion
  106.0 14.1 %fusion = f32[40,256,128]{2,1,0:T(8,128)} fusion(f32[40,512]{1,0:T(8,128)S(1)} %fusion.41, bf16[40,1,512,256]{3,2,0,1:T(8,128)(2,1)} %bitcast.53, bf16[40,256,128]{2,1,0:T(8,128)(2,1)} %gather_fusion, pred[40]{0:T(512)(128)(4,1)S(1)} %compare_and_fusion), kind=kOutput, calls=%fused_computation.2 | convolution fusion | flops 2722365440 | bytes 18432040 | tf_op jit(solution)/shard_map/shct,shtd->schd/dot_general | solution.py:65
  120.1 8.2 %fusion.9 = bf16[32,256,128]{2,0,1:T(8,128)(2,1)S(1)} fusion(f32[40,256,128]{2,1,0:T(8,128)} %fusion, s32[40]{0:T(128)S(1)} %copy-done.4), kind=kOutput, calls=%fused_computation.11 | convolution fusion | flops 504366336 | bytes 7340192 | tf_op jit(solution)/shard_map/su,scw->ucw/dot_general | solution.py:70
  128.4 2.2 copy.15
  130.6 84.1 %reduce-scatter.2.cloned.1.call-done = bf16[1,256,128]{2,1,0:T(8,128)(2,1)} async-done(((bf16[32,256,128]{2,1,0:T(8,128)(2,1)}), bf16[1,256,128]{2,1,0:T(8,128)(2,1)}) %reduce-scatter.2.cloned.1.call-update) | async-done | bytes 65552 | tf_op jit(solution)/shard_map/reduce_scatter | solution.py:71
  214.7 1.5 convert_element_type.44
  216.3 1.0 fusion.35
  217.3 0.1 convert_element_type.38
  217.4 35.5 %all-gather.7.cloned.1.call-done = f32[1,256,1024]{2,1,0:T(8,128)} async-done(((f32[1,256,128]{2,1,0:T(8,128)}), f32[1,256,1024]{2,1,0:T(8,128)}) %all-gather.7.cloned.1.call-update) | async-done | bytes 1048592 | tf_op jit(solution)/shard_map/all_gather | solution.py:76
  253.0 1.4 reduce_sum.48
  254.3 1.5 multiply_reduce_fusion
  255.8 37.5 %all-gather.9.cloned.1.call-done = f32[256,1024]{1,0:T(8,128)} async-done(((f32[256,128]{1,0:T(8,128)}), f32[256,1024]{1,0:T(8,128)}) %all-gather.9.cloned.1.call-update) | async-done | bytes 1048592 | tf_op jit(solution)/shard_map/all_gather | solution.py:77
  293.3 2.5 fusion.15
  (25 shorter events, 0.3 us)
Async XLA Ops:
  6.5 286.8 %copy-start = (bf16[1024,128]{1,0:T(8,128)(2,1)S(1)}, bf16[1024,128]{1,0:T(8,128)(2,1)}, u32[]{:S(2)}) copy-start(bf16[1024,128]{1,0:T(8,128)(2,1)} %param.17) | copy-start | bytes 786436
  6.5 86.7 %all-gather.5.cloned.1.call-start = ((), (), s32[]{:S(2)}) async-start(), calls=%async_computation.1 | async-start | bytes 17301504 | tf_op jit(solution)/shard_map/all_gather | solution.py:40
  11.3 203.4 %reduce-scatter.2.cloned.1.call-start = ((), (), s32[]{:S(2)}) async-start(), calls=%async_computation.2 | async-start | bytes 2162688 | tf_op jit(solution)/shard_map/reduce_scatter | solution.py:71
  106.0 14.1 %copy-start.4 = (s32[40]{0:T(128)S(1)}, s32[40]{0:T(128)}, u32[]{:S(2)}) copy-start(s32[40]{0:T(128)} %param.13) | copy-start | bytes 484
  120.1 96.2 %copy-start.2 = (bf16[1,256,1024]{2,1,0:T(8,128)(2,1)S(1)}, bf16[1,256,1024]{2,1,0:T(8,128)(2,1)}, u32[]{:S(2)}) copy-start(bf16[1,256,1024]{2,1,0:T(8,128)(2,1)} %multiply_convert_fusion.3) | copy-start | bytes 1572868
  120.1 96.2 %copy-start.5 = (bf16[2,1024,128]{2,1,0:T(8,128)(2,1)S(1)}, bf16[2,1024,128]{2,1,0:T(8,128)(2,1)}, u32[]{:S(2)}) copy-start(bf16[2,1024,128]{2,1,0:T(8,128)(2,1)} %param.11) | copy-start | bytes 1572868
  128.4 88.9 %copy-start.1 = (bf16[1,256,1024]{2,1,0:T(8,128)(2,1)S(1)}, bf16[1,256,1024]{2,1,0:T(8,128)(2,1)}, u32[]{:S(2)}) copy-start(bf16[1,256,1024]{2,1,0:T(8,128)(2,1)} %param.9) | copy-start | bytes 1572868
  128.4 165.0 %copy-start.3 = (f32[1024]{0:T(1024)S(1)}, f32[1024]{0:T(1024)}, u32[]{:S(2)}) copy-start(f32[1024]{0:T(1024)} %param.16) | copy-start | bytes 12292
  130.6 122.4 %all-gather.7.cloned.1.call-start = ((), (), s32[]{:S(2)}) async-start(), calls=%async_computation.3 | async-start | bytes 1179648 | tf_op jit(solution)/shard_map/all_gather | solution.py:76
  216.2 77.1 %all-gather.9.cloned.1.call-start = ((), (), s32[]{:S(2)}) async-start(), calls=%async_computation.4 | async-start | bytes 1179648 | tf_op jit(solution)/shard_map/all_gather | solution.py:77
Sparse Core Ops, SparseCore 0:
  11.4 81.7 all-gather.4
  130.7 83.9 reduce-scatter.1
  216.4 36.4 all-gather.6
  254.5 38.7 all-gather.8
where the time goes:
time: 306 us; the launch traced here: 302 us
  waiting for transfers between devices  236 us (77%)
  matrix products  36.1 us (12%)
  between operations  13.2 us (4%)
  other arithmetic  12.6 us (4%)
  local copies, waits for them, and re-layouts  4.72 us (2%)
    reduce_scatter x1, waiting for transfers between devices, local(): lax.psum_scatter(buffer.astype(jnp.bfloat16), 'cand', scatter_dimension=0...  84.1 us
    all_gather x1, waiting for transfers between devices, local(): features = lax.all_gather(normed_input, 'cand', axis=0, tiled=True)  78.4 us
    all_gather x1, waiting for transfers between devices, local(): lax.all_gather(gate_own.astype(jnp.float32).reshape(1, cand_count, head_c...  37.5 us
    all_gather x1, waiting for transfers between devices, local(): lax.all_gather(attn_head, 'hist', axis=2, tiled=True)  35.5 us
    dot_general x1, matrix products, local(): jnp.einsum('shct,shtd->schd', weights, cache_values, preferred_element_ty...  14.1 us
    dot_general x1, matrix products, local(): jnp.dot(features.reshape(user_count * cand_count, D), proj_weight[1], pre...  10.3 us
    dot_general x1, matrix products, local(): jnp.einsum('su,scw->ucw', owner_table, partial_value, precision=lax.Preci...  8.24 us
  transfers between devices with their start and end apart: 4, of which 4 were waited for; matrix products, arithmetic and copies ran while one was open for 2% of the time, Pallas kernels for 0%

commit v1 on v0

v1 whole, which is shorter than its diff:
```python
import functools

import jax
import jax.numpy as jnp
from jax import lax
from jax.experimental import pallas as pl
from jax.experimental.pallas import tpu as pltpu
from jax.sharding import PartitionSpec as P

D = 1024
DH = 128
CANDS = 256
HALF = CANDS // 2
BLK = 512
SLOTS_HERE = 40
USERS = 32
NX, NY, NZ = 4, 4, 8
GROUP = 4
F32 = jnp.float32
BF16 = jnp.bfloat16
MESH = pl.DeviceIdType.MESH
HALF_SCALE = 0.5 * DH ** (-0.5)


def place():
    cand = lax.axis_index("cand")
    return cand // (2 * NY), (cand // 2) % NY, cand % 2, lax.axis_index("hist")


def device(x, y, c, z):
    return (z, (x * NY + y) * 2 + c)


def greet(x, y, c, z):
    barrier = pltpu.get_barrier_semaphore()
    peers = [device(x, y, 1 - c, z)]
    peers += [device((x + d) % NX, y, c, z) for d in range(1, NX)]
    peers += [device(x, (y + d) % NY, c, z) for d in range(1, NY)]
    peers += [device(x, y, c, (z + d) % NZ) for d in range(1, NZ)]
    for peer in peers:
        pl.semaphore_signal(barrier, inc=1, device_id=peer, device_id_type=MESH)
    return barrier, len(peers)


def remote(src, dst, send_sem, recv_sem, peer):
    return pltpu.make_async_remote_copy(
        src_ref=src,
        dst_ref=dst,
        send_sem=send_sem,
        recv_sem=recv_sem,
        device_id=peer,
        device_id_type=MESH,
    )


def silu(value):
    half = 0.5 * value
    return half + half * jnp.tanh(half)


def layer_norm(rows, gain):
    centred = rows - jnp.mean(rows, axis=-1, keepdims=True)
    row_var = jnp.mean(centred * centred, axis=-1, keepdims=True)
    return centred * lax.rsqrt(row_var + 1e-05) * gain


def query_kernel(
    cand_hbm,
    gain_hbm,
    proj_hbm,
    query_all,
    gate_all,
    cand_cols,
    cand_rows,
    gain,
    proj,
    normed,
    load_sem,
    line_send,
    line_recv,
    cross_send,
    cross_recv,
    core_send,
    core_recv,
    gate_send,
    gate_recv,
):
    x, y, c, z = place()
    barrier, greeted = greet(x, y, c, z)
    loads = [
        pltpu.make_async_copy(cand_hbm.at[0], cand_rows, load_sem.at[0]),
        pltpu.make_async_copy(gain_hbm, gain, load_sem.at[1]),
        pltpu.make_async_copy(proj_hbm, proj, load_sem.at[2]),
    ]
    for load in loads:
        load.start()
    loads[0].wait()
    loads[1].wait()
    for part in range(4):
        rows = pl.ds(part * 64, 64)
        normed[rows, :] = layer_norm(cand_rows[rows, :].astype(F32), gain[...]).astype(BF16)
    loads[2].wait()
    query_all[x, y, c] = silu(
        jnp.dot(normed[...], proj[1], preferred_element_type=F32)
    ).astype(BF16)
    pl.semaphore_wait(barrier, greeted)

    halves = [pl.ds(0, HALF), pl.ds(HALF, HALF)]
    sends = []
    line = [[], []]
    for d in (2, 1, 3):
        for h in range(2):
            peer = device((x + d) % NX, y, c, z) if h == 0 else device(x, (y + d) % NY, c, z)
            own = query_all.at[x, y, c, halves[h]]
            copy = remote(own, own, line_send.at[h, d], line_recv.at[h, d], peer)
            copy.start()
            line[h].append(copy)
            sends.append(copy)

    gate_all[z] = silu(
        jnp.dot(normed[...], proj[0], preferred_element_type=F32)
    ).astype(BF16)
    gates = []
    for d in (4, 3, 5, 2, 6, 1, 7):
        own = gate_all.at[z]
        copy = remote(
            own, own, gate_send.at[d], gate_recv.at[d], device(x, y, c, (z + d) % NZ)
        )
        copy.start()
        gates.append(copy)
        sends.append(copy)

    cand_cols[...] = cand_rows[:, pl.ds(pl.multiple_of(z * DH, DH), DH)]

    cross = [[], []]
    core = []

    def to_core(index, block):
        copy = remote(
            block, block, core_send.at[index], core_recv.at[index], device(x, y, 1 - c, z)
        )
        copy.start()
        core.append(copy)
        sends.append(copy)

    for h in range(2):
        for copy in line[h]:
            copy.wait_recv()
        for d in (2, 1, 3):
            if h == 0:
                block = query_all.at[:, y, c, halves[h]]
                peer = device(x, (y + d) % NY, c, z)
            else:
                block = query_all.at[x, :, c, halves[h]]
                peer = device((x + d) % NX, y, c, z)
            copy = remote(block, block, cross_send.at[h, d], cross_recv.at[h, d], peer)
            copy.start()
            cross[h].append((d, copy))
            sends.append(copy)
        to_core(h, block)

    for turn in (1, 2, 0):
        for h in range(2):
            d, copy = cross[h][turn]
            copy.wait_recv()
            if h == 0:
                block = query_all.at[:, (y + NY - d) % NY, c, halves[h]]
            else:
                block = query_all.at[(x + NX - d) % NX, :, c, halves[h]]
            to_core(2 + 2 * turn + h, block)
    for copy in gates:
        copy.wait_recv()
    for copy in core:
        copy.wait_recv()
    for copy in sends:
        copy.wait_send()


def attention_kernel(
    user_hbm,
    block_hbm,
    length_hbm,
    query_all,
    cache_hbm,
    partial,
    total,
    cache,
    user_ref,
    block_ref,
    length_ref,
    slots,
    counts,
    load_sem,
    sems,
):
    loads = [
        pltpu.make_async_copy(user_hbm, user_ref, load_sem.at[0]),
        pltpu.make_async_copy(block_hbm, block_ref, load_sem.at[1]),
        pltpu.make_async_copy(length_hbm, length_ref, load_sem.at[2]),
    ]
    for load in loads:
        load.start()
    for load in loads:
        load.wait()

    def find(slot, found):
        user = user_ref[slot]
        block = block_ref[slot]
        count = jnp.clip(length_ref[user] - block * BLK, 0, BLK)
        live = (block >= 0) & (count > 0)

        @pl.when(live)
        def _():
            slots[found] = slot
            counts[found] = count
            pltpu.make_async_copy(cache_hbm.at[slot, 0], cache.at[slot], sems.at[slot]).start()

        return found + live.astype(jnp.int32)

    found = lax.fori_loop(0, SLOTS_HERE, find, 0)
    for extra in range(GROUP - 1):
        slots[found + extra] = slots[0]
        counts[found + extra] = 0

    def clear(user, _):
        total[user] = jnp.zeros((CANDS, DH), F32)
        return 0

    lax.fori_loop(0, USERS, clear, 0)
    event = lax.broadcasted_iota(jnp.int32, (1, BLK), 1)

    def group(first, _):
        for step in range(GROUP):
            entry = first * GROUP + step
            slot = slots[entry]

            @pl.when(entry < found)
            def _(slot=slot):
                pltpu.make_async_copy(cache_hbm.at[slot, 0], cache.at[slot], sems.at[slot]).wait()

        sums = []
        for step in range(GROUP):
            entry = first * GROUP + step
            slot = slots[entry]
            user = user_ref[slot]
            scale = jnp.where(event < counts[entry], HALF_SCALE, 0.0)
            scores = lax.dot_general(
                query_all[user],
                cache[slot, :, :DH],
                (((1,), (1,)), ((), ())),
                preferred_element_type=F32,
            )
            half = scores * scale
            weights = (half + half * jnp.tanh(half)).astype(BF16)
            sums.append(
                (user, jnp.dot(weights, cache[slot, :, DH:], preferred_element_type=F32))
            )
        for user, value in sums:
            total[user] += value
        return 0

    lax.fori_loop(0, (found + GROUP - 1) // GROUP, group, 0)

    def store(user, _):
        partial[user] = total[user].astype(BF16)
        return 0

    lax.fori_loop(0, USERS, store, 0)


def output_kernel(
    partial,
    gate_all,
    cand_cols,
    gain_hbm,
    weight_hbm,
    result,
    core_in,
    cross_out,
    cross_in,
    line_out,
    line_in,
    attention,
    gain,
    weight,
    load_sem,
    core_send,
    core_recv,
    cross_send,
    cross_recv,
    line_send,
    line_recv,
    head_send,
    head_recv,
):
    x, y, c, z = place()
    barrier, greeted = greet(x, y, c, z)
    loads = [
        pltpu.make_async_copy(gain_hbm, gain, load_sem.at[0]),
        pltpu.make_async_copy(weight_hbm, weight, load_sem.at[1]),
    ]
    for load in loads:
        load.start()
    pl.semaphore_wait(barrier, greeted)

    halves = [pl.ds(0, HALF), pl.ds(HALF, HALF)]
    sends = []
    core = {}

    def lot(h, d, core_index):
        if h == 0:
            return partial.at[:, (y + d) % NY, core_index, halves[h]]
        return partial.at[(x + d) % NX, :, core_index, halves[h]]

    order = (2, 1, 3, 0)
    for d in order:
        for h in range(2):
            copy = remote(
                lot(h, d, 1 - c),
                core_in.at[h, d],
                core_send.at[h, d],
                core_recv.at[h, d],
                device(x, y, 1 - c, z),
            )
            copy.start()
            core[h, d] = copy
            sends.append(copy)
    cross = {}
    for d in order:
        for h in range(2):
            core[h, d].wait_recv()
            summed = lot(h, d, c)[...].astype(F32) + core_in[h, d].astype(F32)
            cross_out[h, d] = summed.astype(BF16)
            if d:
                peer = device(x, (y + d) % NY, c, z) if h == 0 else device((x + d) % NX, y, c, z)
                copy = remote(
                    cross_out.at[h, d],
                    cross_in.at[h, d],
                    cross_send.at[h, d],
                    cross_recv.at[h, d],
                    peer,
                )
                copy.start()
                cross[h, d] = copy
                sends.append(copy)
    line = {}
    for h in range(2):
        for d in (1, 3, 2):
            cross[h, d].wait_recv()
        own = x if h == 0 else y
        for d in order:
            other = (own + d) % NX
            value = cross_out[h, 0, other].astype(F32)
            for e in range(1, NX):
                value += cross_in[h, e, other].astype(F32)
            line_out[h, d] = value.astype(BF16)
            if d:
                peer = device(other, y, c, z) if h == 0 else device(x, other, c, z)
                copy = remote(
                    line_out.at[h, d],
                    line_in.at[h, d],
                    line_send.at[h, d],
                    line_recv.at[h, d],
                    peer,
                )
                copy.start()
                line[h, d] = copy
                sends.append(copy)
    head = {}
    for h in range(2):
        value = line_out[h, 0].astype(F32)
        for d in (1, 3, 2):
            line[h, d].wait_recv()
            value += line_in[h, d].astype(F32)
        attention[h, z] = value.astype(BF16)
        for d in (4, 3, 5, 2, 6, 1, 7):
            own = attention.at[h, z]
            copy = remote(
                own, own, head_send.at[h, d], head_recv.at[h, d], device(x, y, c, (z + d) % NZ)
            )
            copy.start()
            head[h, d] = copy
            sends.append(copy)
    for load in loads:
        load.wait()
    for h in range(2):
        for d in range(1, NZ):
            head[h, d].wait_recv()
        for part in range(2):
            rows = pl.ds(part * 64, 64)
            out_rows = pl.ds(h * HALF + part * 64, 64)
            whole = jnp.concatenate(
                [attention[h, k, rows].astype(F32) for k in range(NZ)], axis=1
            )
            gates = jnp.concatenate(
                [gate_all[k, out_rows].astype(F32) for k in range(NZ)], axis=1
            )
            gated = (layer_norm(whole, gain[...]) * gates).astype(BF16)
            projected = jnp.dot(gated, weight[...], preferred_element_type=F32)
            result[0, out_rows, :] = (cand_cols[out_rows, :].astype(F32) + projected).astype(BF16)
    for copy in sends:
        copy.wait_send()


def local(
    candidates,
    input_gain,
    proj_weight,
    history_cache,
    slot_user,
    slot_block,
    history_len,
    attention_gain,
    out_weight,
):
    dma = pltpu.SemaphoreType.DMA
    vmem = pl.BlockSpec(memory_space=pltpu.VMEM)
    anywhere = pl.BlockSpec(memory_space=pl.ANY)
    in_hbm = functools.partial(pltpu.with_memory_space_constraint, memory_space=pltpu.HBM)
    query_all, gate_all, cand_cols = pl.pallas_call(
        query_kernel,
        out_shape=[
            pltpu.VMEM((NX, NY, 2, CANDS, DH), BF16),
            pltpu.VMEM((NZ, CANDS, DH), BF16),
            pltpu.VMEM((CANDS, DH), BF16),
        ],
        in_specs=[anywhere] * 3,
        out_specs=[vmem] * 3,
        scratch_shapes=[
            pltpu.VMEM((CANDS, D), BF16),
            pltpu.VMEM((1, D), F32),
            pltpu.VMEM((2, D, DH), BF16),
            pltpu.VMEM((CANDS, D), BF16),
            dma((3,)),
            dma((2, NX)),
            dma((2, NX)),
            dma((2, NX)),
            dma((2, NX)),
            dma((8,)),
            dma((8,)),
            dma((NZ,)),
            dma((NZ,)),
        ],
        compiler_params=pltpu.CompilerParams(
            collective_id=0, has_side_effects=True, vmem_limit_bytes=24 << 20
        ),
        name="query",
    )(in_hbm(candidates), in_hbm(input_gain.reshape(1, D)), in_hbm(proj_weight))

    partial = pl.pallas_call(
        attention_kernel,
        out_shape=pltpu.VMEM((USERS, CANDS, DH), BF16),
        in_specs=[anywhere] * 3 + [vmem, anywhere],
        out_specs=vmem,
        scratch_shapes=[
            pltpu.VMEM((USERS, CANDS, DH), F32),
            pltpu.VMEM((SLOTS_HERE, BLK, 2 * DH), BF16),
            pltpu.SMEM((SLOTS_HERE,), jnp.int32),
            pltpu.SMEM((SLOTS_HERE,), jnp.int32),
            pltpu.SMEM((USERS,), jnp.int32),
            pltpu.SMEM((SLOTS_HERE + GROUP,), jnp.int32),
            pltpu.SMEM((SLOTS_HERE + GROUP,), jnp.int32),
            dma((3,)),
            dma((SLOTS_HERE,)),
        ],
        compiler_params=pltpu.CompilerParams(vmem_limit_bytes=32 << 20),
        name="attention",
    )(
        in_hbm(slot_user),
        in_hbm(slot_block),
        in_hbm(history_len),
        query_all.reshape(USERS, CANDS, DH),
        in_hbm(history_cache),
    )

    return pl.pallas_call(
        output_kernel,
        out_shape=jax.ShapeDtypeStruct((1, CANDS, DH), BF16),
        in_specs=[vmem] * 3 + [anywhere] * 2,
        out_specs=vmem,
        scratch_shapes=[
            pltpu.VMEM((2, NX, NX, HALF, DH), BF16),
            pltpu.VMEM((2, NX, NX, HALF, DH), BF16),
            pltpu.VMEM((2, NX, NX, HALF, DH), BF16),
            pltpu.VMEM((2, NX, HALF, DH), BF16),
            pltpu.VMEM((2, NX, HALF, DH), BF16),
            pltpu.VMEM((2, NZ, HALF, DH), BF16),
            pltpu.VMEM((1, D), F32),
            pltpu.VMEM((D, DH), BF16),
            dma((2,)),
            dma((2, NX)),
            dma((2, NX)),
            dma((2, NX)),
            dma((2, NX)),
            dma((2, NX)),
            dma((2, NX)),
            dma((2, NZ)),
            dma((2, NZ)),
        ],
        compiler_params=pltpu.CompilerParams(
            collective_id=1, has_side_effects=True, vmem_limit_bytes=24 << 20
        ),
        name="output",
    )(
        partial.reshape(NX, NY, 2, CANDS, DH),
        gate_all,
        cand_cols,
        in_hbm(attention_gain.reshape(1, D)),
        in_hbm(out_weight),
    )


def solution(mesh):
    return jax.shard_map(
        local,
        mesh=mesh,
        in_specs=(
            P("cand", None, None),
            P(),
            P(None, None, "hist"),
            P("cand", "hist", None, None),
            P("cand"),
            P("cand"),
            P(),
            P(),
            P(None, "hist"),
        ),
        out_specs=P("cand", None, "hist"),
        check_vma=False,
    )
```

time: 306 us -> 63.3 us (0.21); the launches traced: 302 us -> 63.2 us
  waiting for transfers between devices: 236 us -> 0 us
  Pallas kernels: 0 us -> 62.5 us
  matrix products: 36.1 us -> 0 us
  between operations: 13.2 us -> 0.02 us
  other arithmetic: 12.6 us -> 0 us
  local copies, waits for them, and re-layouts: 4.72 us -> 0.63 us
    all_gather x3 -> x0, waiting for transfers between devices: 151 us -> none  [the longest x1 78.4 us: local(): features = lax.all_gather(normed_input, 'cand', axis=0, tiled=True)]
    reduce_scatter x1 -> x0, waiting for transfers between devices: 84.1 us -> none  [local(): lax.psum_scatter(buffer.astype(jnp.bfloat16), 'cand', scatter_dimension=0...]
    pallas_call x0 -> x3, Pallas kernels: none -> 62.5 us  [the longest x1 29.2 us: local(): pl.pallas_call(output_kernel, out_shape=jax.ShapeDtypeStruct((1, CANDS, D...]
    dot_general x5 -> x0, matrix products: 36.1 us -> none  [the longest x1 14.1 us: local(): jnp.einsum('shct,shtd->schd', weights, cache_values, preferred_element_ty...]
    reduce_sum x5 -> x0, other arithmetic: 6.14 us -> none  [the longest x2 2.79 us: layer_norm(): row_var = jnp.mean(centred * centred, axis=-1, keepdims=True)]
    convert_element_type x4 -> x0, other arithmetic: 3.84 us -> none  [the longest x1 2.13 us: local(): normed_input = layer_norm(cand_rows, input_gain).astype(jnp.bfloat16)]
  transfers between devices with their start and end apart: 4 -> 0, of which waited for: 4 -> 0; matrix products, arithmetic and copies ran while one was open for 2% -> 0% of each run, Pallas kernels for 0% -> 0%
where the time goes in v1:
time: 63.3 us; the launch traced here: 63.2 us
  Pallas kernels  62.5 us (99%)
    pallas_call x1, Pallas kernels, local(): pl.pallas_call(output_kernel, out_shape=jax.ShapeDtypeStruct((1, CANDS, D...  29.2 us
    pallas_call x1, Pallas kernels, local(): pl.pallas_call(query_kernel, out_shape=[pltpu.VMEM((NX, NY, 2, CANDS, DH)...  24.3 us
    pallas_call x1, Pallas kernels, local(): pl.pallas_call(attention_kernel, out_shape=pltpu.VMEM((USERS, CANDS, DH),...  9.06 us

profile of v1, /device:TPU:1, one launch (start us, length us, event | category | flops | bytes accessed | tf_op | source)
XLA Modules:
  0.0 63.2 jit_solution(2225651167641816855)
XLA Ops:
  0.0 24.3 %query.1 = (bf16[4,4,2,256,128]{4,3,2,1,0:T(8,128)(2,1)S(1)}, bf16[8,256,128]{2,1,0:T(8,128)(2,1)S(1)}, bf16[256,128]{1,0:T(8,128)(2,1)S(1)}) custom-call(bf16[1,256,1024]{2,1,0:T(8,128)(2,1)} %cand_hbm.1, f32[1,1024]{1,0:T(1,128)} %bitcast.6, bf16[2,1024,128]{2,1,0:T(8,128)(2,1)} %proj_hbm.1), custom_call_target="tpu_custom_call" | custom-call | tf_op jit(solution)/shard_map/query/pallas_call | solution.py:420
  24.3 9.1 %attention.1 = bf16[32,256,128]{2,1,0:T(8,128)(2,1)S(1)} custom-call(s32[40]{0:T(128)} %user_hbm.1, s32[40]{0:T(128)} %block_hbm.1, s32[32]{0:T(128)} %length_hbm.1, bf16[32,256,128]{2,1,0:T(8,128)(2,1)S(1)} %bitcast.5, bf16[40,1,512,256]{3,2,1,0:T(8,128)(2,1)} %cache_hbm.1), custom_call_target="tpu_custom_call" | custom-call | tf_op jit(solution)/shard_map/attention/pallas_call | solution.py:450
  33.4 29.2 %output.1 = bf16[1,256,128]{2,1,0:T(8,128)(2,1)S(1)} custom-call(bf16[4,4,2,256,128]{4,3,2,1,0:T(8,128)(2,1)S(1)} %bitcast.4, bf16[8,256,128]{2,1,0:T(8,128)(2,1)S(1)} %get-tuple-element.9.gate_all, bf16[256,128]{1,0:T(8,128)(2,1)S(1)} %get-tuple-element.10.cand_cols, f32[1,1024]{1,0:T(1,128)} %bitcast.7, bf16[1024,128]{1,0:T(8,128)(2,1)} %weight_hbm.1), custom_call_target="tpu_custom_call" | custom-call | tf_op jit(solution)/shard_map/output/pallas_call | solution.py:476
  62.5 0.6 %copy.11 = bf16[1,256,128]{2,1,0:T(8,128)(2,1)} copy(bf16[1,256,128]{2,1,0:T(8,128)(2,1)S(1)} %output.1) | data formatting | bytes 131072

commit v2 on v0

v2 whole, which is shorter than its diff:
```python
import functools

import jax
import jax.numpy as jnp
from jax import lax
from jax.experimental import pallas as pl
from jax.experimental.pallas import tpu as pltpu
from jax.sharding import PartitionSpec as P

D = 1024
DH = 128
CANDS = 256
HALF = CANDS // 2
QUARTER = CANDS // 4
BLK = 512
TILE = 256
SLOTS_HERE = 40
USERS = 32
NX, NY, NZ = 4, 4, 8
UNROLL = 4
ROUNDS = SLOTS_HERE // (2 * UNROLL)
F32 = jnp.float32
BF16 = jnp.bfloat16
I32 = jnp.int32
MESH = pl.DeviceIdType.MESH
HALF_SCALE = 0.5 * DH ** (-0.5)
FAR_FIRST = (2, 1, 3, 0)
HEADS_FAR_FIRST = (4, 3, 5, 2, 6, 1, 7)
SLOT, OWNER, COUNT, SAME, LAST = range(5)


def place():
    cand = lax.axis_index("cand")
    return cand // (2 * NY), (cand // 2) % NY, cand % 2, lax.axis_index("hist")


def device(x, y, c, z):
    return (z, (x * NY + y) * 2 + c)


def remote(src, dst, send_sem, recv_sem, peer):
    return pltpu.make_async_remote_copy(
        src_ref=src,
        dst_ref=dst,
        send_sem=send_sem,
        recv_sem=recv_sem,
        device_id=peer,
        device_id_type=MESH,
    )


def silu(value):
    half = 0.5 * value
    return half + half * jnp.tanh(half)


def layer_norm(rows, gain):
    centred = rows - jnp.mean(rows, axis=-1, keepdims=True)
    row_var = jnp.mean(centred * centred, axis=-1, keepdims=True)
    return centred * lax.rsqrt(row_var + 1e-05) * gain


def sort_slots(user_row, block_row, length_row, table):
    shape = (SLOTS_HERE, SLOTS_HERE)
    row_id = lax.broadcasted_iota(I32, shape, 0)
    col_id = lax.broadcasted_iota(I32, shape, 1)
    diagonal = row_id == col_id
    slot = lax.broadcasted_iota(I32, (SLOTS_HERE, 1), 0)
    user_id = lax.broadcasted_iota(I32, (SLOTS_HERE, USERS), 1)

    def across(mask, value):
        return jnp.sum(jnp.where(mask, value, 0), axis=1, keepdims=True)

    def down(mask, value):
        return jnp.sum(jnp.where(mask, value, 0), axis=0, keepdims=True)

    user = across(diagonal, user_row)
    block = across(diagonal, block_row)
    length = across(user_id == user, length_row)
    count = jnp.clip(length - block * BLK, 0, BLK)
    live = (block >= 0) & (count > 0)
    key = jnp.where(live, user * SLOTS_HERE, USERS * SLOTS_HERE) + slot
    key_row = down(diagonal, key)
    rank = across(key_row < key, 1)
    here = rank == col_id
    owner = down(here, user)
    before = down(rank + 1 == col_id, user + 1)
    through = down(live & (user <= user_id), 1)
    mine = down(live & (user == user_id), 1)
    table[...] = jnp.zeros_like(table)
    table[SLOT : SLOT + 1, :SLOTS_HERE] = down(here, slot)
    table[OWNER : OWNER + 1, :SLOTS_HERE] = owner
    table[COUNT : COUNT + 1, :SLOTS_HERE] = down(here, jnp.where(live, count, 0))
    table[SAME : SAME + 1, :SLOTS_HERE] = (before == owner + 1).astype(I32)
    table[LAST : LAST + 1, :USERS] = jnp.where(mine > 0, through - 1, SLOTS_HERE)


def attend(table, query, cache, sums, total, first, last):
    event = lax.broadcasted_iota(I32, (1, BLK), 1)
    blank = jnp.zeros((HALF, DH), BF16)

    def weigh(scores, scale):
        half = scores * scale
        return (half + half * jnp.tanh(half)).astype(BF16)

    def step(round_id, _):
        for turn in range(UNROLL):
            entry = (round_id * UNROLL + turn) * 2
            slot_a, slot_b = table[SLOT, entry], table[SLOT, entry + 1]
            scale_a = jnp.where(event < table[COUNT, entry], HALF_SCALE, 0.0)
            scale_b = jnp.where(event < table[COUNT, entry + 1], HALF_SCALE, 0.0)
            queries = jnp.concatenate(
                [
                    jnp.concatenate([query[table[OWNER, entry]], blank], axis=1),
                    jnp.concatenate([blank, query[table[OWNER, entry + 1]]], axis=1),
                ],
                axis=0,
            )
            value = jnp.zeros((2 * HALF, 2 * DH), F32)
            for tile in range(BLK // TILE):
                cols = slice(tile * TILE, (tile + 1) * TILE)
                keys = jnp.concatenate(
                    [cache[slot_a, cols, :DH], cache[slot_b, cols, :DH]], axis=1
                )
                values = jnp.concatenate(
                    [cache[slot_a, cols, DH:], cache[slot_b, cols, DH:]], axis=1
                )
                scores = lax.dot_general(
                    queries, keys, (((1,), (1,)), ((), ())), preferred_element_type=F32
                )
                weights = jnp.concatenate(
                    [weigh(scores[:HALF], scale_a[:, cols]), weigh(scores[HALF:], scale_b[:, cols])],
                    axis=0,
                )
                value += jnp.dot(weights, values, preferred_element_type=F32)
            run = total[...] * table[SAME, entry].astype(F32) + value[:HALF, :DH]
            sums[entry] = run.astype(BF16)
            run = run * table[SAME, entry + 1].astype(F32) + value[HALF:, DH:]
            sums[entry + 1] = run.astype(BF16)
            total[...] = run
        return 0

    lax.fori_loop(first, last, step, 0)


def kernel(
    cand_hbm,
    input_gain_hbm,
    proj_hbm,
    cache_hbm,
    user_hbm,
    block_hbm,
    length_hbm,
    attention_gain_hbm,
    weight_hbm,
    result,
    cand_rows,
    input_gain,
    proj,
    cache,
    user_row,
    block_row,
    length_row,
    attention_gain,
    weight,
    normed,
    query_a,
    query_b,
    gate_all,
    table_rows,
    table,
    sums_a,
    sums_b,
    total,
    core_out,
    core_in,
    peer_out,
    peer_in,
    attention,
    load_sem,
    line_send,
    line_recv,
    cross_send,
    cross_recv,
    share_send,
    share_recv,
    gate_send,
    gate_recv,
    core_send,
    core_recv,
    peer_send,
    peer_recv,
    head_send,
    head_recv,
):
    x, y, c, z = place()
    barrier = pltpu.get_barrier_semaphore()
    peers = [device(x, y, 1 - c, z)]
    peers += [
        device((x + dx) % NX, (y + dy) % NY, c, z)
        for dx in range(NX)
        for dy in range(NY)
        if dx or dy
    ]
    peers += [device(x, y, c, (z + d) % NZ) for d in range(1, NZ)]
    for peer in peers:
        pl.semaphore_signal(barrier, inc=1, device_id=peer, device_id_type=MESH)

    pairs = [
        (cand_hbm.at[0], cand_rows),
        (input_gain_hbm, input_gain),
        (proj_hbm, proj),
        (user_hbm, user_row),
        (block_hbm, block_row),
        (length_hbm, length_row),
        (cache_hbm.at[:, 0], cache),
        (attention_gain_hbm, attention_gain),
        (weight_hbm, weight),
    ]
    loads = [
        pltpu.make_async_copy(src, dst, load_sem.at[i]) for i, (src, dst) in enumerate(pairs)
    ]
    for load in loads:
        load.start()

    query = (query_a, query_b)
    sums = (sums_a, sums_b)
    halves = (pl.ds(0, HALF), pl.ds(HALF, HALF))
    quarters = (pl.ds(0, QUARTER), pl.ds(QUARTER, QUARTER))
    sends = []

    def go(src, dst, send_sem, recv_sem, peer):
        copy = remote(src, dst, send_sem, recv_sem, peer)
        copy.start()
        sends.append(copy)
        return copy

    def project_query(h):
        for part in range(2):
            rows = pl.ds(h * HALF + part * QUARTER, QUARTER)
            normed[rows, :] = layer_norm(
                cand_rows[rows, :].astype(F32), input_gain[...]
            ).astype(BF16)
        if h == 0:
            loads[2].wait()
        query[h][x, y, c] = silu(
            jnp.dot(normed[halves[h], :], proj[1], preferred_element_type=F32)
        ).astype(BF16)

    line, cross, share = {}, {}, {}

    def send_line(h):
        for d in (2, 1, 3):
            for s in range(2):
                peer = device((x + d) % NX, y, c, z) if s == 0 else device(x, (y + d) % NY, c, z)
                own = query[h].at[x, y, c, quarters[s]]
                line[h, s, d] = go(own, own, line_send.at[h, s, d], line_recv.at[h, s, d], peer)

    def to_core(h, index, block):
        share[h, index] = go(
            block,
            block,
            share_send.at[h, index],
            share_recv.at[h, index],
            device(x, y, 1 - c, z),
        )

    def send_cross(h):
        for s in range(2):
            for d in (1, 3, 2):
                line[h, s, d].wait_recv()
            block = (
                query[h].at[:, y, c, quarters[s]] if s == 0 else query[h].at[x, :, c, quarters[s]]
            )
            for d in (2, 1, 3):
                peer = device(x, (y + d) % NY, c, z) if s == 0 else device((x + d) % NX, y, c, z)
                cross[h, s, d] = go(
                    block, block, cross_send.at[h, s, d], cross_recv.at[h, s, d], peer
                )
            to_core(h, s * NX, block)

    def share_cross(h):
        for d in (1, 3, 2):
            for s in range(2):
                cross[h, s, d].wait_recv()
                if s == 0:
                    block = query[h].at[:, (y + NY - d) % NY, c, quarters[s]]
                else:
                    block = query[h].at[(x + NX - d) % NX, :, c, quarters[s]]
                to_core(h, s * NX + d, block)

    def wait_query(h):
        for index in range(2 * NX):
            share[h, index].wait_recv()

    loads[0].wait()
    loads[1].wait()
    project_query(0)
    pl.semaphore_wait(barrier, len(peers))
    send_line(0)
    project_query(1)
    send_line(1)
    gate_all[z] = silu(jnp.dot(normed[...], proj[0], preferred_element_type=F32)).astype(BF16)
    gates = []
    for d in HEADS_FAR_FIRST:
        own = gate_all.at[z]
        gates.append(
            go(own, own, gate_send.at[d], gate_recv.at[d], device(x, y, c, (z + d) % NZ))
        )
    for index in range(3, 6):
        loads[index].wait()
    sort_slots(user_row[...], block_row[...], length_row[...], table_rows)
    to_scalars = pltpu.make_async_copy(table_rows, table, load_sem.at[len(pairs)])
    to_scalars.start()
    send_cross(0)
    send_cross(1)
    for h in range(2):
        sums[h][SLOTS_HERE] = jnp.zeros((HALF, DH), BF16)
    total[...] = jnp.zeros((HALF, DH), F32)
    to_scalars.wait()
    loads[6].wait()
    share_cross(0)
    wait_query(0)

    core, peer_copies = {}, {}

    def chip_user(kx, ky, which):
        return (kx * NY + ky) * 2 + which

    def send_core(h):
        for dx in FAR_FIRST:
            kx = (x + dx) % NX
            for ky in range(NY):
                core_out[h, kx, ky] = sums[h][table[LAST, chip_user(kx, ky, 1 - c)]]
            core[h, dx] = go(
                core_out.at[h, kx],
                core_in.at[h, kx],
                core_send.at[h, dx],
                core_recv.at[h, dx],
                device(x, y, 1 - c, z),
            )

    def send_peers(h):
        for dx in FAR_FIRST:
            core[h, dx].wait_recv()
            kx = (x + dx) % NX
            for dy in FAR_FIRST:
                ky = (y + dy) % NY
                mine = sums[h][table[LAST, chip_user(kx, ky, c)]].astype(F32)
                offset = dx * NY + dy
                peer_out[h, offset] = (mine + core_in[h, kx, ky].astype(F32)).astype(BF16)
                if offset:
                    peer_copies[h, offset] = go(
                        peer_out.at[h, offset],
                        peer_in.at[h, offset],
                        peer_send.at[h, offset],
                        peer_recv.at[h, offset],
                        device(kx, ky, c, z),
                    )

    head = {}

    def send_heads(h):
        value = peer_out[h, 0].astype(F32)
        for offset in range(1, NX * NY):
            peer_copies[h, offset].wait_recv()
            value += peer_in[h, offset].astype(F32)
        attention[h, z] = value.astype(BF16)
        for d in HEADS_FAR_FIRST:
            own = attention.at[h, z]
            head[h, d] = go(
                own, own, head_send.at[h, d], head_recv.at[h, d], device(x, y, c, (z + d) % NZ)
            )

    def finish(h):
        for d in range(1, NZ):
            head[h, d].wait_recv()
        for part in range(2):
            rows = pl.ds(part * QUARTER, QUARTER)
            out_rows = pl.ds(h * HALF + part * QUARTER, QUARTER)
            whole = jnp.concatenate([attention[h, k, rows].astype(F32) for k in range(NZ)], axis=1)
            gate = jnp.concatenate([gate_all[k, out_rows].astype(F32) for k in range(NZ)], axis=1)
            gated = (layer_norm(whole, attention_gain[...]) * gate).astype(BF16)
            projected = jnp.dot(gated, weight[...], preferred_element_type=F32)
            cols = cand_rows[out_rows, pl.ds(pl.multiple_of(z * DH, DH), DH)].astype(F32)
            result[0, out_rows, :] = (cols + projected).astype(BF16)

    attend(table, query_a.reshape(USERS, HALF, DH), cache, sums_a, total, 0, ROUNDS - 1)
    share_cross(1)
    attend(table, query_a.reshape(USERS, HALF, DH), cache, sums_a, total, ROUNDS - 1, ROUNDS)
    send_core(0)
    wait_query(1)
    total[...] = jnp.zeros((HALF, DH), F32)
    attend(table, query_b.reshape(USERS, HALF, DH), cache, sums_b, total, 0, 1)
    send_peers(0)
    attend(table, query_b.reshape(USERS, HALF, DH), cache, sums_b, total, 1, ROUNDS)
    send_core(1)
    send_peers(1)
    send_heads(0)
    send_heads(1)
    loads[7].wait()
    loads[8].wait()
    for copy in gates:
        copy.wait_recv()
    finish(0)
    finish(1)
    for copy in sends:
        copy.wait_send()


def local(
    candidates,
    input_gain,
    proj_weight,
    history_cache,
    slot_user,
    slot_block,
    history_len,
    attention_gain,
    out_weight,
):
    dma = pltpu.SemaphoreType.DMA
    vmem = pltpu.VMEM
    operands = (
        candidates,
        input_gain.reshape(1, D),
        proj_weight,
        history_cache,
        slot_user.reshape(1, SLOTS_HERE),
        slot_block.reshape(1, SLOTS_HERE),
        history_len.reshape(1, USERS),
        attention_gain.reshape(1, D),
        out_weight,
    )
    return pl.pallas_call(
        kernel,
        out_shape=jax.ShapeDtypeStruct((1, CANDS, DH), BF16),
        in_specs=[pl.BlockSpec(memory_space=pl.ANY)] * len(operands),
        out_specs=pl.BlockSpec(memory_space=vmem),
        scratch_shapes=[
            vmem((CANDS, D), BF16),
            vmem((1, D), F32),
            vmem((2, D, DH), BF16),
            vmem((SLOTS_HERE, BLK, 2 * DH), BF16),
            vmem((1, SLOTS_HERE), I32),
            vmem((1, SLOTS_HERE), I32),
            vmem((1, USERS), I32),
            vmem((1, D), F32),
            vmem((D, DH), BF16),
            vmem((CANDS, D), BF16),
            vmem((NX, NY, 2, HALF, DH), BF16),
            vmem((NX, NY, 2, HALF, DH), BF16),
            vmem((NZ, CANDS, DH), BF16),
            vmem((8, 128), I32),
            pltpu.SMEM((8, 128), I32),
            vmem((SLOTS_HERE + 1, HALF, DH), BF16),
            vmem((SLOTS_HERE + 1, HALF, DH), BF16),
            vmem((HALF, DH), F32),
            vmem((2, NX, NY, HALF, DH), BF16),
            vmem((2, NX, NY, HALF, DH), BF16),
            vmem((2, NX * NY, HALF, DH), BF16),
            vmem((2, NX * NY, HALF, DH), BF16),
            vmem((2, NZ, HALF, DH), BF16),
            dma((len(operands) + 1,)),
            dma((2, 2, NX)),
            dma((2, 2, NX)),
            dma((2, 2, NX)),
            dma((2, 2, NX)),
            dma((2, 2 * NX)),
            dma((2, 2 * NX)),
            dma((NZ,)),
            dma((NZ,)),
            dma((2, NX)),
            dma((2, NX)),
            dma((2, NX * NY)),
            dma((2, NX * NY)),
            dma((2, NZ)),
            dma((2, NZ)),
        ],
        compiler_params=pltpu.CompilerParams(
            collective_id=0, has_side_effects=True, vmem_limit_bytes=48 << 20
        ),
        name="layer",
    )(*[pltpu.with_memory_space_constraint(operand, pltpu.HBM) for operand in operands])


def solution(mesh):
    return jax.shard_map(
        local,
        mesh=mesh,
        in_specs=(
            P("cand", None, None),
            P(),
            P(None, None, "hist"),
            P("cand", "hist", None, None),
            P("cand"),
            P("cand"),
            P(),
            P(),
            P(None, "hist"),
        ),
        out_specs=P("cand", None, "hist"),
        check_vma=False,
    )
```

time: 306 us -> 53.2 us (0.17); the launches traced: 302 us -> 53.1 us
  waiting for transfers between devices: 236 us -> 0 us
  Pallas kernels: 0 us -> 52.5 us
  matrix products: 36.1 us -> 0 us
  between operations: 13.2 us -> 0.01 us
  other arithmetic: 12.6 us -> 0 us
  local copies, waits for them, and re-layouts: 4.72 us -> 0.63 us
    all_gather x3 -> x0, waiting for transfers between devices: 151 us -> none  [the longest x1 78.4 us: local(): features = lax.all_gather(normed_input, 'cand', axis=0, tiled=True)]
    reduce_scatter x1 -> x0, waiting for transfers between devices: 84.1 us -> none  [local(): lax.psum_scatter(buffer.astype(jnp.bfloat16), 'cand', scatter_dimension=0...]
    pallas_call x0 -> x1, Pallas kernels: none -> 52.5 us  [local(): pl.pallas_call(kernel, out_shape=jax.ShapeDtypeStruct((1, CANDS, DH), BF1...]
    dot_general x5 -> x0, matrix products: 36.1 us -> none  [the longest x1 14.1 us: local(): jnp.einsum('shct,shtd->schd', weights, cache_values, preferred_element_ty...]
    reduce_sum x5 -> x0, other arithmetic: 6.14 us -> none  [the longest x2 2.79 us: layer_norm(): row_var = jnp.mean(centred * centred, axis=-1, keepdims=True)]
    convert_element_type x4 -> x0, other arithmetic: 3.84 us -> none  [the longest x1 2.13 us: local(): normed_input = layer_norm(cand_rows, input_gain).astype(jnp.bfloat16)]
  transfers between devices with their start and end apart: 4 -> 0, of which waited for: 4 -> 0; matrix products, arithmetic and copies ran while one was open for 2% -> 0% of each run, Pallas kernels for 0% -> 0%
where the time goes in v2:
time: 53.2 us; the launch traced here: 53.1 us
  Pallas kernels  52.5 us (99%)
  local copies, waits for them, and re-layouts  0.63 us (1%)
    pallas_call x1, Pallas kernels, local(): pl.pallas_call(kernel, out_shape=jax.ShapeDtypeStruct((1, CANDS, DH), BF1...  52.5 us

profile of v2, /device:TPU:1, one launch (start us, length us, event | category | flops | bytes accessed | tf_op | source)
XLA Modules:
  0.0 53.1 jit_solution(13418402787572020729)
XLA Ops:
  0.0 52.5 %layer.1 = bf16[1,256,128]{2,1,0:T(8,128)(2,1)S(1)} custom-call(bf16[1,256,1024]{2,1,0:T(8,128)(2,1)} %cand_hbm.1, f32[1,1024]{1,0:T(1,128)} %bitcast.5, bf16[2,1024,128]{2,1,0:T(8,128)(2,1)} %proj_hbm.1, bf16[40,1,512,256]{3,2,1,0:T(8,128)(2,1)} %cache_hbm.1, s32[1,40]{1,0:T(1,128)} %bitcast.7, s32[1,40]{1,0:T(1,128)} %bitcast.8, s32[1,32]{1,0:T(1,128)} %bitcast.9, ...), custom_call_target="tpu_custom_call" | custom-call | tf_op jit(solution)/shard_map/layer/pallas_call | solution.py:435
  52.5 0.6 %copy.11 = bf16[1,256,128]{2,1,0:T(8,128)(2,1)} copy(bf16[1,256,128]{2,1,0:T(8,128)(2,1)S(1)} %layer.1) | data formatting | bytes 131072

commit v3 on v2

--- a/solution.py
+++ b/solution.py
@@ -178,38 +178,33 @@
     peer_in,
     attention,
     load_sem,
-    line_send,
     line_recv,
-    cross_send,
     cross_recv,
-    share_send,
     share_recv,
-    gate_send,
     gate_recv,
-    core_send,
     core_recv,
-    peer_send,
     peer_recv,
-    head_send,
     head_recv,
+    send_sem,
 ):
     x, y, c, z = place()
+    xs = [lax.rem(x + d, NX) for d in range(NX)]
+    ys = [lax.rem(y + d, NY) for d in range(NY)]
+    zs = [lax.rem(z + d, NZ) for d in range(NZ)]
+    sibling = device(x, y, 1 - c, z)
     barrier = pltpu.get_barrier_semaphore()
-    peers = [device(x, y, 1 - c, z)]
+    peers = [sibling]
     peers += [
-        device((x + dx) % NX, (y + dy) % NY, c, z)
-        for dx in range(NX)
-        for dy in range(NY)
-        if dx or dy
+        device(xs[dx], ys[dy], c, z) for dx in range(NX) for dy in range(NY) if dx or dy
     ]
-    peers += [device(x, y, c, (z + d) % NZ) for d in range(1, NZ)]
-    for peer in peers:
-        pl.semaphore_signal(barrier, inc=1, device_id=peer, device_id_type=MESH)
-
+    peers += [device(x, y, c, zs[d]) for d in range(1, NZ)]
+    halves = (pl.ds(0, HALF), pl.ds(HALF, HALF))
     pairs = [
-        (cand_hbm.at[0], cand_rows),
+        (cand_hbm.at[0, halves[0]], cand_rows.at[halves[0]]),
         (input_gain_hbm, input_gain),
-        (proj_hbm, proj),
+        (proj_hbm.at[1], proj.at[1]),
+        (cand_hbm.at[0, halves[1]], cand_rows.at[halves[1]]),
+        (proj_hbm.at[0], proj.at[0]),
         (user_hbm, user_row),
         (block_hbm, block_row),
         (length_hbm, length_row),
@@ -220,22 +215,28 @@
     loads = [
         pltpu.make_async_copy(src, dst, load_sem.at[i]) for i, (src, dst) in enumerate(pairs)
     ]
-    for load in loads:
+    for load in loads[:8]:
         load.start()
+    for peer in peers:
+        pl.semaphore_signal(barrier, inc=1, device_id=peer, device_id_type=MESH)
 
     query = (query_a, query_b)
     sums = (sums_a, sums_b)
-    halves = (pl.ds(0, HALF), pl.ds(HALF, HALF))
     quarters = (pl.ds(0, QUARTER), pl.ds(QUARTER, QUARTER))
-    sends = []
-
-    def go(src, dst, send_sem, recv_sem, peer):
-        copy = remote(src, dst, send_sem, recv_sem, peer)
-        copy.start()
-        sends.append(copy)
-        return copy
+    LINE, CROSS, SHARE, CORE, PEER, HEAD = (0, 2, 4, 6, 8, 10)
+    GATE = 12
+
+    def go(src, dst, group, recv_sem, peer):
+        remote(src, dst, send_sem.at[group], recv_sem, peer).start()
+
+    def arrived(ref, recv_sem):
+        remote(ref, ref, send_sem.at[0], recv_sem, sibling).wait_recv()
+
+    def sent(ref, group):
+        remote(ref, ref, send_sem.at[group], gate_recv.at[0], sibling).wait_send()
 
     def project_query(h):
+        loads[3 * h].wait()
         for part in range(2):
             rows = pl.ds(h * HALF + part * QUARTER, QUARTER)
             normed[rows, :] = layer_norm(
@@ -247,68 +248,55 @@
             jnp.dot(normed[halves[h], :], proj[1], preferred_element_type=F32)
         ).astype(BF16)
 
-    line, cross, share = {}, {}, {}
-
     def send_line(h):
         for d in (2, 1, 3):
             for s in range(2):
-                peer = device((x + d) % NX, y, c, z) if s == 0 else device(x, (y + d) % NY, c, z)
+                peer = device(xs[d], y, c, z) if s == 0 else device(x, ys[d], c, z)
                 own = query[h].at[x, y, c, quarters[s]]
-                line[h, s, d] = go(own, own, line_send.at[h, s, d], line_recv.at[h, s, d], peer)
-
-    def to_core(h, index, block):
-        share[h, index] = go(
-            block,
-            block,
-            share_send.at[h, index],
-            share_recv.at[h, index],
-            device(x, y, 1 - c, z),
-        )
+                go(own, own, LINE + h, line_recv.at[h, s], peer)
+
+    def to_core(h, block):
+        go(block, block, SHARE + h, share_recv.at[h], sibling)
 
     def send_cross(h):
         for s in range(2):
-            for d in (1, 3, 2):
-                line[h, s, d].wait_recv()
+            arrived(query[h].at[pl.ds(0, NX - 1), 0, 0, quarters[s]], line_recv.at[h, s])
             block = (
                 query[h].at[:, y, c, quarters[s]] if s == 0 else query[h].at[x, :, c, quarters[s]]
             )
             for d in (2, 1, 3):
-                peer = device(x, (y + d) % NY, c, z) if s == 0 else device((x + d) % NX, y, c, z)
-                cross[h, s, d] = go(
-                    block, block, cross_send.at[h, s, d], cross_recv.at[h, s, d], peer
-                )
-            to_core(h, s * NX, block)
+                peer = device(x, ys[d], c, z) if s == 0 else device(xs[d], y, c, z)
+                go(block, block, CROSS + h, cross_recv.at[h, s, d - 1], peer)
+            to_core(h, block)
 
     def share_cross(h):
         for d in (1, 3, 2):
             for s in range(2):
-                cross[h, s, d].wait_recv()
                 if s == 0:
-                    block = query[h].at[:, (y + NY - d) % NY, c, quarters[s]]
+                    block = query[h].at[:, ys[NY - d], c, quarters[s]]
                 else:
-                    block = query[h].at[(x + NX - d) % NX, :, c, quarters[s]]
-                to_core(h, s * NX + d, block)
+                    block = query[h].at[xs[NX - d], :, c, quarters[s]]
+                arrived(block, cross_recv.at[h, s, d - 1])
+                to_core(h, block)
 
     def wait_query(h):
-        for index in range(2 * NX):
-            share[h, index].wait_recv()
-
-    loads[0].wait()
+        arrived(query[h].at[:, :, 0], share_recv.at[h])
+
     loads[1].wait()
     project_query(0)
     pl.semaphore_wait(barrier, len(peers))
     send_line(0)
     project_query(1)
     send_line(1)
+    loads[4].wait()
     gate_all[z] = silu(jnp.dot(normed[...], proj[0], preferred_element_type=F32)).astype(BF16)
-    gates = []
     for d in HEADS_FAR_FIRST:
         own = gate_all.at[z]
-        gates.append(
-            go(own, own, gate_send.at[d], gate_recv.at[d], device(x, y, c, (z + d) % NZ))
-        )
-    for index in range(3, 6):
-        loads[index].wait()
+        go(own, own, GATE, gate_recv.at[0], device(x, y, c, zs[d]))
+    for load in loads[8:]:
+        load.start()
+    for load in loads[5:8]:
+        load.wait()
     sort_slots(user_row[...], block_row[...], length_row[...], table_rows)
     to_scalars = pltpu.make_async_copy(table_rows, table, load_sem.at[len(pairs)])
     to_scalars.start()
@@ -318,94 +306,97 @@
         sums[h][SLOTS_HERE] = jnp.zeros((HALF, DH), BF16)
     total[...] = jnp.zeros((HALF, DH), F32)
     to_scalars.wait()
-    loads[6].wait()
+    loads[8].wait()
     share_cross(0)
     wait_query(0)
 
-    core, peer_copies = {}, {}
-
     def chip_user(kx, ky, which):
         return (kx * NY + ky) * 2 + which
 
     def send_core(h):
         for dx in FAR_FIRST:
-            kx = (x + dx) % NX
+            kx = xs[dx]
             for ky in range(NY):
                 core_out[h, kx, ky] = sums[h][table[LAST, chip_user(kx, ky, 1 - c)]]
-            core[h, dx] = go(
-                core_out.at[h, kx],
-                core_in.at[h, kx],
-                core_send.at[h, dx],
-                core_recv.at[h, dx],
-                device(x, y, 1 - c, z),
-            )
-
-    def send_peers(h):
+            go(core_out.at[h, kx], core_in.at[h, kx], CORE + h, core_recv.at[h, dx], sibling)
+
+    def send_peers(h, p, first):
         for dx in FAR_FIRST:
-            core[h, dx].wait_recv()
-            kx = (x + dx) % NX
+            kx = xs[dx]
+            if first:
+                arrived(core_in.at[h, kx], core_recv.at[h, dx])
             for dy in FAR_FIRST:
-                ky = (y + dy) % NY
-                mine = sums[h][table[LAST, chip_user(kx, ky, c)]].astype(F32)
+                mine = sums[h][table[LAST, chip_user(kx, ys[dy], c)], quarters[p]]
+                peer_out[h, dx * NY + dy, quarters[p]] = mine + core_in[h, kx, ys[dy], quarters[p]]
+            for dy in FAR_FIRST:
                 offset = dx * NY + dy
-                peer_out[h, offset] = (mine + core_in[h, kx, ky].astype(F32)).astype(BF16)
                 if offset:
-                    peer_copies[h, offset] = go(
-                        peer_out.at[h, offset],
-                        peer_in.at[h, offset],
-                        peer_send.at[h, offset],
-                        peer_recv.at[h, offset],
-                        device(kx, ky, c, z),
+                    go(
+                        peer_out.at[h, offset, quarters[p]],
+                        peer_in.at[h, offset, quarters[p]],
+                        PEER + h,
+                        peer_recv.at[h, p],
+                        device(kx, ys[dy], c, z),
                     )
 
-    head = {}
-
-    def send_heads(h):
-        value = peer_out[h, 0].astype(F32)
+    def send_heads(h, p):
+        others = pl.ds(1, NX * NY - 1)
+        arrived(peer_in.at[h, others, quarters[p]], peer_recv.at[h, p])
+        value = peer_out[h, 0, quarters[p]].astype(F32)
         for offset in range(1, NX * NY):
-            peer_copies[h, offset].wait_recv()
-            value += peer_in[h, offset].astype(F32)
-        attention[h, z] = value.astype(BF16)
+            value += peer_in[h, offset, quarters[p]].astype(F32)
+        attention[h, z, quarters[p]] = value.astype(BF16)
+        own = attention.at[h, z, quarters[p]]
         for d in HEADS_FAR_FIRST:
-            own = attention.at[h, z]
-            head[h, d] = go(
-                own, own, head_send.at[h, d], head_recv.at[h, d], device(x, y, c, (z + d) % NZ)
-            )
-
-    def finish(h):
-        for d in range(1, NZ):
-            head[h, d].wait_recv()
-        for part in range(2):
-            rows = pl.ds(part * QUARTER, QUARTER)
-            out_rows = pl.ds(h * HALF + part * QUARTER, QUARTER)
-            whole = jnp.concatenate([attention[h, k, rows].astype(F32) for k in range(NZ)], axis=1)
-            gate = jnp.concatenate([gate_all[k, out_rows].astype(F32) for k in range(NZ)], axis=1)
-            gated = (layer_norm(whole, attention_gain[...]) * gate).astype(BF16)
-            projected = jnp.dot(gated, weight[...], preferred_element_type=F32)
-            cols = cand_rows[out_rows, pl.ds(pl.multiple_of(z * DH, DH), DH)].astype(F32)
-            result[0, out_rows, :] = (cols + projected).astype(BF16)
-
-    attend(table, query_a.reshape(USERS, HALF, DH), cache, sums_a, total, 0, ROUNDS - 1)
+            go(own, own, HEAD + h, head_recv.at[h, p], device(x, y, c, zs[d]))
+
+    def finish(h, p):
+        arrived(attention.at[h, pl.ds(0, NZ - 1), quarters[p]], head_recv.at[h, p])
+        out_rows = pl.ds(h * HALF + p * QUARTER, QUARTER)
+        whole = jnp.concatenate(
+            [attention[h, k, quarters[p]].astype(F32) for k in range(NZ)], axis=1
+        )
+        gate = jnp.concatenate([gate_all[k, out_rows].astype(F32) for k in range(NZ)], axis=1)
+        gated = (layer_norm(whole, attention_gain[...]) * gate).astype(BF16)
+        projected = jnp.dot(gated, weight[...], preferred_element_type=F32)
+        cols = cand_rows[out_rows, pl.ds(pl.multiple_of(z * DH, DH), DH)].astype(F32)
+        result[0, out_rows, :] = (cols + projected).astype(BF16)
+
+    flat_a = query_a.reshape(USERS, HALF, DH)
+    flat_b = query_b.reshape(USERS, HALF, DH)
+    attend(table, flat_a, cache, sums_a, total, 0, 3)
     share_cross(1)
-    attend(table, query_a.reshape(USERS, HALF, DH), cache, sums_a, total, ROUNDS - 1, ROUNDS)
+    attend(table, flat_a, cache, sums_a, total, 3, ROUNDS)
     send_core(0)
     wait_query(1)
     total[...] = jnp.zeros((HALF, DH), F32)
-    attend(table, query_b.reshape(USERS, HALF, DH), cache, sums_b, total, 0, 1)
-    send_peers(0)
-    attend(table, query_b.reshape(USERS, HALF, DH), cache, sums_b, total, 1, ROUNDS)
+    attend(table, flat_b, cache, sums_b, total, 0, 1)
+    send_peers(0, 0, True)
+    attend(table, flat_b, cache, sums_b, total, 1, 2)
+    send_peers(0, 1, False)
+    attend(table, flat_b, cache, sums_b, total, 2, ROUNDS)
     send_core(1)
-    send_peers(1)
-    send_heads(0)
-    send_heads(1)
-    loads[7].wait()
-    loads[8].wait()
-    for copy in gates:
-        copy.wait_recv()
-    finish(0)
-    finish(1)
-    for copy in sends:
-        copy.wait_send()
+    send_heads(0, 0)
+    send_peers(1, 0, True)
+    send_peers(1, 1, False)
+    send_heads(0, 1)
+    send_heads(1, 0)
+    loads[9].wait()
+    loads[10].wait()
+    arrived(gate_all.at[pl.ds(0, NZ - 1)], gate_recv.at[0])
+    finish(0, 0)
+    finish(0, 1)
+    send_heads(1, 1)
+    finish(1, 0)
+    finish(1, 1)
+    for h in range(2):
+        sent(query[h].at[pl.ds(0, NX - 1), 0, 0], LINE + h)
+        sent(query[h].at[pl.ds(0, NX - 1), :, 0], CROSS + h)
+        sent(query[h].at[:, :, 0], SHARE + h)
+        sent(core_out.at[h], CORE + h)
+        sent(peer_out.at[h, pl.ds(1, NX * NY - 1)], PEER + h)
+        sent(attention.at[h, pl.ds(0, NZ - 1)], HEAD + h)
+    sent(gate_all.at[pl.ds(0, NZ - 1)], GATE)
 
 
 def local(
@@ -461,21 +452,15 @@
             vmem((2, NX * NY, HALF, DH), BF16),
             vmem((2, NX * NY, HALF, DH), BF16),
             vmem((2, NZ, HALF, DH), BF16),
-            dma((len(operands) + 1,)),
-            dma((2, 2, NX)),
-            dma((2, 2, NX)),
-            dma((2, 2, NX)),
-            dma((2, 2, NX)),
-            dma((2, 2 * NX)),
-            dma((2, 2 * NX)),
-            dma((NZ,)),
-            dma((NZ,)),
+            dma((len(operands) + 3,)),
+            dma((2, 2)),
+            dma((2, 2, NX - 1)),
+            dma((2,)),
+            dma((1,)),
             dma((2, NX)),
-            dma((2, NX)),
-            dma((2, NX * NY)),
-            dma((2, NX * NY)),
-            dma((2, NZ)),
-            dma((2, NZ)),
+            dma((2, 2)),
+            dma((2, 2)),
+            dma((13,)),
         ],
         compiler_params=pltpu.CompilerParams(
             collective_id=0, has_side_effects=True, vmem_limit_bytes=48 << 20

time: 53.2 us -> 49.3 us (0.927)
  Pallas kernels: 52.5 us -> 48.3 us
    pallas_call x1, Pallas kernels: 52.5 us -> 48.3 us  [local(): pl.pallas_call(kernel, out_shape=jax.ShapeDtypeStruct((1, CANDS, DH), BF1...]
where the time goes in v3:
time: 49.3 us; the launch traced here: 48.9 us
  Pallas kernels  48.3 us (98%)
  local copies, waits for them, and re-layouts  0.63 us (1%)
    pallas_call x1, Pallas kernels, local(): pl.pallas_call(kernel, out_shape=jax.ShapeDtypeStruct((1, CANDS, DH), BF1...  48.3 us

profile of v3, /device:TPU:1, one launch (start us, length us, event | category | flops | bytes accessed | tf_op | source)
XLA Modules:
  0.0 48.9 jit_solution(5225341935720335086)
XLA Ops:
  0.0 48.3 %layer.1 = bf16[1,256,128]{2,1,0:T(8,128)(2,1)S(1)} custom-call(bf16[1,256,1024]{2,1,0:T(8,128)(2,1)} %cand_hbm.1, f32[1,1024]{1,0:T(1,128)} %bitcast.5, bf16[2,1024,128]{2,1,0:T(8,128)(2,1)} %proj_hbm.1, bf16[40,1,512,256]{3,2,1,0:T(8,128)(2,1)} %cache_hbm.1, s32[1,40]{1,0:T(1,128)} %bitcast.7, s32[1,40]{1,0:T(1,128)} %bitcast.8, s32[1,32]{1,0:T(1,128)} %bitcast.9, ...), custom_call_target="tpu_custom_call" | custom-call | tf_op jit(solution)/shard_map/layer/pallas_call | solution.py:426
  48.3 0.6 %copy.11 = bf16[1,256,128]{2,1,0:T(8,128)(2,1)} copy(bf16[1,256,128]{2,1,0:T(8,128)(2,1)S(1)} %layer.1) | data formatting | bytes 131072

commit v4 on v3

--- a/solution.py
+++ b/solution.py
@@ -25,6 +25,7 @@
 MESH = pl.DeviceIdType.MESH
 HALF_SCALE = 0.5 * DH ** (-0.5)
 FAR_FIRST = (2, 1, 3, 0)
+PARTS = (2, 4)
 HEADS_FAR_FIRST = (4, 3, 5, 2, 6, 1, 7)
 SLOT, OWNER, COUNT, SAME, LAST = range(5)
 
@@ -301,61 +302,71 @@
     to_scalars = pltpu.make_async_copy(table_rows, table, load_sem.at[len(pairs)])
     to_scalars.start()
     send_cross(0)
-    send_cross(1)
     for h in range(2):
         sums[h][SLOTS_HERE] = jnp.zeros((HALF, DH), BF16)
     total[...] = jnp.zeros((HALF, DH), F32)
     to_scalars.wait()
     loads[8].wait()
     share_cross(0)
+    send_cross(1)
     wait_query(0)
 
     def chip_user(kx, ky, which):
         return (kx * NY + ky) * 2 + which
 
-    def send_core(h):
+    def part(h, p):
+        size = HALF // PARTS[h]
+        return pl.ds(p * size, size)
+
+    def send_core(h, p):
+        rows = part(h, p)
+        for kx in range(NX):
+            for ky in range(NY):
+                user = chip_user(kx, ky, 1 - c)
+                core_out[h, kx, ky, rows] = sums[h][table[LAST, user], rows]
+        go(
+            core_out.at[h, :, :, rows],
+            core_in.at[h, :, :, rows],
+            CORE + h,
+            core_recv.at[h, p],
+            sibling,
+        )
+
+    def send_peers(h, p):
+        rows = part(h, p)
+        arrived(core_in.at[h, :, :, rows], core_recv.at[h, p])
         for dx in FAR_FIRST:
             kx = xs[dx]
-            for ky in range(NY):
-                core_out[h, kx, ky] = sums[h][table[LAST, chip_user(kx, ky, 1 - c)]]
-            go(core_out.at[h, kx], core_in.at[h, kx], CORE + h, core_recv.at[h, dx], sibling)
-
-    def send_peers(h, p, first):
-        for dx in FAR_FIRST:
-            kx = xs[dx]
-            if first:
-                arrived(core_in.at[h, kx], core_recv.at[h, dx])
             for dy in FAR_FIRST:
-                mine = sums[h][table[LAST, chip_user(kx, ys[dy], c)], quarters[p]]
-                peer_out[h, dx * NY + dy, quarters[p]] = mine + core_in[h, kx, ys[dy], quarters[p]]
+                mine = sums[h][table[LAST, chip_user(kx, ys[dy], c)], rows]
+                peer_out[h, dx * NY + dy, rows] = mine + core_in[h, kx, ys[dy], rows]
             for dy in FAR_FIRST:
                 offset = dx * NY + dy
                 if offset:
                     go(
-                        peer_out.at[h, offset, quarters[p]],
-                        peer_in.at[h, offset, quarters[p]],
+                        peer_out.at[h, offset, rows],
+                        peer_in.at[h, offset, rows],
                         PEER + h,
                         peer_recv.at[h, p],
                         device(kx, ys[dy], c, z),
                     )
 
     def send_heads(h, p):
-        others = pl.ds(1, NX * NY - 1)
-        arrived(peer_in.at[h, others, quarters[p]], peer_recv.at[h, p])
-        value = peer_out[h, 0, quarters[p]].astype(F32)
+        rows = part(h, p)
+        arrived(peer_in.at[h, pl.ds(1, NX * NY - 1), rows], peer_recv.at[h, p])
+        value = peer_out[h, 0, rows].astype(F32)
         for offset in range(1, NX * NY):
-            value += peer_in[h, offset, quarters[p]].astype(F32)
-        attention[h, z, quarters[p]] = value.astype(BF16)
-        own = attention.at[h, z, quarters[p]]
+            value += peer_in[h, offset, rows].astype(F32)
+        attention[h, z, rows] = value.astype(BF16)
+        own = attention.at[h, z, rows]
         for d in HEADS_FAR_FIRST:
             go(own, own, HEAD + h, head_recv.at[h, p], device(x, y, c, zs[d]))
 
     def finish(h, p):
-        arrived(attention.at[h, pl.ds(0, NZ - 1), quarters[p]], head_recv.at[h, p])
-        out_rows = pl.ds(h * HALF + p * QUARTER, QUARTER)
-        whole = jnp.concatenate(
-            [attention[h, k, quarters[p]].astype(F32) for k in range(NZ)], axis=1
-        )
+        rows = part(h, p)
+        arrived(attention.at[h, pl.ds(0, NZ - 1), rows], head_recv.at[h, p])
+        out_rows = pl.ds(h * HALF + rows.start, rows.size)
+        whole = jnp.concatenate([attention[h, k, rows].astype(F32) for k in range(NZ)], axis=1)
         gate = jnp.concatenate([gate_all[k, out_rows].astype(F32) for k in range(NZ)], axis=1)
         gated = (layer_norm(whole, attention_gain[...]) * gate).astype(BF16)
         projected = jnp.dot(gated, weight[...], preferred_element_type=F32)
@@ -367,28 +378,34 @@
     attend(table, flat_a, cache, sums_a, total, 0, 3)
     share_cross(1)
     attend(table, flat_a, cache, sums_a, total, 3, ROUNDS)
-    send_core(0)
+    send_core(0, 0)
+    send_core(0, 1)
     wait_query(1)
     total[...] = jnp.zeros((HALF, DH), F32)
     attend(table, flat_b, cache, sums_b, total, 0, 1)
-    send_peers(0, 0, True)
+    send_peers(0, 0)
     attend(table, flat_b, cache, sums_b, total, 1, 2)
-    send_peers(0, 1, False)
+    send_peers(0, 1)
     attend(table, flat_b, cache, sums_b, total, 2, ROUNDS)
-    send_core(1)
+    for p in range(PARTS[1]):
+        send_core(1, p)
     send_heads(0, 0)
-    send_peers(1, 0, True)
-    send_peers(1, 1, False)
+    send_peers(1, 0)
+    send_peers(1, 1)
     send_heads(0, 1)
-    send_heads(1, 0)
+    send_peers(1, 2)
+    send_peers(1, 3)
     loads[9].wait()
     loads[10].wait()
     arrived(gate_all.at[pl.ds(0, NZ - 1)], gate_recv.at[0])
     finish(0, 0)
+    send_heads(1, 0)
+    send_heads(1, 1)
+    send_heads(1, 2)
     finish(0, 1)
-    send_heads(1, 1)
-    finish(1, 0)
-    finish(1, 1)
+    send_heads(1, 3)
+    for p in range(PARTS[1]):
+        finish(1, p)
     for h in range(2):
         sent(query[h].at[pl.ds(0, NX - 1), 0, 0], LINE + h)
         sent(query[h].at[pl.ds(0, NX - 1), :, 0], CROSS + h)
@@ -457,9 +474,9 @@
             dma((2, 2, NX - 1)),
             dma((2,)),
             dma((1,)),
-            dma((2, NX)),
-            dma((2, 2)),
-            dma((2, 2)),
+            dma((2, 4)),
+            dma((2, 4)),
+            dma((2, 4)),
             dma((13,)),
         ],
         compiler_params=pltpu.CompilerParams(

time: 49.3 us -> 47.7 us (0.968)
  Pallas kernels: 48.3 us -> 47 us
    pallas_call x1, Pallas kernels: 48.3 us -> 47 us  [local(): pl.pallas_call(kernel, out_shape=jax.ShapeDtypeStruct((1, CANDS, DH), BF1...]
where the time goes in v4:
time: 47.7 us; the launch traced here: 47.6 us
  Pallas kernels  47 us (99%)
  local copies, waits for them, and re-layouts  0.63 us (1%)
    pallas_call x1, Pallas kernels, local(): pl.pallas_call(kernel, out_shape=jax.ShapeDtypeStruct((1, CANDS, DH), BF1...  47 us

profile of v4, /device:TPU:1, one launch (start us, length us, event | category | flops | bytes accessed | tf_op | source)
XLA Modules:
  0.0 47.6 jit_solution(16524788488675830500)
XLA Ops:
  0.0 47.0 %layer.1 = bf16[1,256,128]{2,1,0:T(8,128)(2,1)S(1)} custom-call(bf16[1,256,1024]{2,1,0:T(8,128)(2,1)} %cand_hbm.1, f32[1,1024]{1,0:T(1,128)} %bitcast.5, bf16[2,1024,128]{2,1,0:T(8,128)(2,1)} %proj_hbm.1, bf16[40,1,512,256]{3,2,1,0:T(8,128)(2,1)} %cache_hbm.1, s32[1,40]{1,0:T(1,128)} %bitcast.7, s32[1,40]{1,0:T(1,128)} %bitcast.8, s32[1,32]{1,0:T(1,128)} %bitcast.9, ...), custom_call_target="tpu_custom_call" | custom-call | tf_op jit(solution)/shard_map/layer/pallas_call | solution.py:443
  47.0 0.6 %copy.11 = bf16[1,256,128]{2,1,0:T(8,128)(2,1)} copy(bf16[1,256,128]{2,1,0:T(8,128)(2,1)S(1)} %layer.1) | data formatting | bytes 131072

commit v5 on v4

--- a/solution.py
+++ b/solution.py
@@ -224,17 +224,11 @@
     query = (query_a, query_b)
     sums = (sums_a, sums_b)
     quarters = (pl.ds(0, QUARTER), pl.ds(QUARTER, QUARTER))
-    LINE, CROSS, SHARE, CORE, PEER, HEAD = (0, 2, 4, 6, 8, 10)
-    GATE = 12
-
-    def go(src, dst, group, recv_sem, peer):
-        remote(src, dst, send_sem.at[group], recv_sem, peer).start()
+    def go(src, dst, recv_sem, peer):
+        remote(src, dst, send_sem.at[0], recv_sem, peer).start()
 
     def arrived(ref, recv_sem):
         remote(ref, ref, send_sem.at[0], recv_sem, sibling).wait_recv()
-
-    def sent(ref, group):
-        remote(ref, ref, send_sem.at[group], gate_recv.at[0], sibling).wait_send()
 
     def project_query(h):
         loads[3 * h].wait()
@@ -254,10 +248,10 @@
             for s in range(2):
                 peer = device(xs[d], y, c, z) if s == 0 else device(x, ys[d], c, z)
                 own = query[h].at[x, y, c, quarters[s]]
-                go(own, own, LINE + h, line_recv.at[h, s], peer)
+                go(own, own, line_recv.at[h, s], peer)
 
     def to_core(h, block):
-        go(block, block, SHARE + h, share_recv.at[h], sibling)
+        go(block, block, share_recv.at[h], sibling)
 
     def send_cross(h):
         for s in range(2):
@@ -267,7 +261,7 @@
             )
             for d in (2, 1, 3):
                 peer = device(x, ys[d], c, z) if s == 0 else device(xs[d], y, c, z)
-                go(block, block, CROSS + h, cross_recv.at[h, s, d - 1], peer)
+                go(block, block, cross_recv.at[h, s, d - 1], peer)
             to_core(h, block)
 
     def share_cross(h):
@@ -293,7 +287,7 @@
     gate_all[z] = silu(jnp.dot(normed[...], proj[0], preferred_element_type=F32)).astype(BF16)
     for d in HEADS_FAR_FIRST:
         own = gate_all.at[z]
-        go(own, own, GATE, gate_recv.at[0], device(x, y, c, zs[d]))
+        go(own, own, gate_recv.at[0], device(x, y, c, zs[d]))
     for load in loads[8:]:
         load.start()
     for load in loads[5:8]:
@@ -327,14 +321,13 @@
         go(
             core_out.at[h, :, :, rows],
             core_in.at[h, :, :, rows],
-            CORE + h,
-            core_recv.at[h, p],
+            core_recv.at[PARTS[0] * h + p],
             sibling,
         )
 
     def send_peers(h, p):
         rows = part(h, p)
-        arrived(core_in.at[h, :, :, rows], core_recv.at[h, p])
+        arrived(core_in.at[h, :, :, rows], core_recv.at[PARTS[0] * h + p])
         for dx in FAR_FIRST:
             kx = xs[dx]
             for dy in FAR_FIRST:
@@ -346,25 +339,24 @@
                     go(
                         peer_out.at[h, offset, rows],
                         peer_in.at[h, offset, rows],
-                        PEER + h,
-                        peer_recv.at[h, p],
+                        peer_recv.at[PARTS[0] * h + p],
                         device(kx, ys[dy], c, z),
                     )
 
     def send_heads(h, p):
         rows = part(h, p)
-        arrived(peer_in.at[h, pl.ds(1, NX * NY - 1), rows], peer_recv.at[h, p])
+        arrived(peer_in.at[h, pl.ds(1, NX * NY - 1), rows], peer_recv.at[PARTS[0] * h + p])
         value = peer_out[h, 0, rows].astype(F32)
         for offset in range(1, NX * NY):
             value += peer_in[h, offset, rows].astype(F32)
         attention[h, z, rows] = value.astype(BF16)
         own = attention.at[h, z, rows]
         for d in HEADS_FAR_FIRST:
-            go(own, own, HEAD + h, head_recv.at[h, p], device(x, y, c, zs[d]))
+            go(own, own, head_recv.at[PARTS[0] * h + p], device(x, y, c, zs[d]))
 
     def finish(h, p):
         rows = part(h, p)
-        arrived(attention.at[h, pl.ds(0, NZ - 1), rows], head_recv.at[h, p])
+        arrived(attention.at[h, pl.ds(0, NZ - 1), rows], head_recv.at[PARTS[0] * h + p])
         out_rows = pl.ds(h * HALF + rows.start, rows.size)
         whole = jnp.concatenate([attention[h, k, rows].astype(F32) for k in range(NZ)], axis=1)
         gate = jnp.concatenate([gate_all[k, out_rows].astype(F32) for k in range(NZ)], axis=1)
@@ -406,14 +398,8 @@
     send_heads(1, 3)
     for p in range(PARTS[1]):
         finish(1, p)
-    for h in range(2):
-        sent(query[h].at[pl.ds(0, NX - 1), 0, 0], LINE + h)
-        sent(query[h].at[pl.ds(0, NX - 1), :, 0], CROSS + h)
-        sent(query[h].at[:, :, 0], SHARE + h)
-        sent(core_out.at[h], CORE + h)
-        sent(peer_out.at[h, pl.ds(1, NX * NY - 1)], PEER + h)
-        sent(attention.at[h, pl.ds(0, NZ - 1)], HEAD + h)
-    sent(gate_all.at[pl.ds(0, NZ - 1)], GATE)
+    whole = cache.at[pl.ds(0, 19)]
+    remote(whole, whole, send_sem.at[0], gate_recv.at[0], sibling).wait_send()
 
 
 def local(
@@ -474,10 +460,10 @@
             dma((2, 2, NX - 1)),
             dma((2,)),
             dma((1,)),
-            dma((2, 4)),
-            dma((2, 4)),
-            dma((2, 4)),
-            dma((13,)),
+            dma((sum(PARTS),)),
+            dma((sum(PARTS),)),
+            dma((sum(PARTS),)),
+            dma((1,)),
         ],
         compiler_params=pltpu.CompilerParams(
             collective_id=0, has_side_effects=True, vmem_limit_bytes=48 << 20

time: 47.7 us -> 47.5 us (level)
  no operation moved by 1% of the time
where the time goes in v5:
time: 47.5 us; the launch traced here: 47.4 us
  Pallas kernels  46.8 us (99%)
  local copies, waits for them, and re-layouts  0.63 us (1%)
    pallas_call x1, Pallas kernels, local(): pl.pallas_call(kernel, out_shape=jax.ShapeDtypeStruct((1, CANDS, DH), BF1...  46.8 us

profile of v5, /device:TPU:1, one launch (start us, length us, event | category | flops | bytes accessed | tf_op | source)
XLA Modules:
  0.0 47.4 jit_solution(871285456866958306)
XLA Ops:
  0.0 46.8 %layer.1 = bf16[1,256,128]{2,1,0:T(8,128)(2,1)S(1)} custom-call(bf16[1,256,1024]{2,1,0:T(8,128)(2,1)} %cand_hbm.1, f32[1,1024]{1,0:T(1,128)} %bitcast.5, bf16[2,1024,128]{2,1,0:T(8,128)(2,1)} %proj_hbm.1, bf16[40,1,512,256]{3,2,1,0:T(8,128)(2,1)} %cache_hbm.1, s32[1,40]{1,0:T(1,128)} %bitcast.7, s32[1,40]{1,0:T(1,128)} %bitcast.8, s32[1,32]{1,0:T(1,128)} %bitcast.9, ...), custom_call_target="tpu_custom_call" | custom-call | tf_op jit(solution)/shard_map/layer/pallas_call | solution.py:429
  46.8 0.6 %copy.11 = bf16[1,256,128]{2,1,0:T(8,128)(2,1)} copy(bf16[1,256,128]{2,1,0:T(8,128)(2,1)S(1)} %layer.1) | data formatting | bytes 131072
